TPU v7x, 32 devices: a whole 2x2x4 slice. The times are simulated.
32 devices in a mesh: seq: 8 (over z, y), mp: 4 (over x, core).
Axes of the slice: x: 2, y: 2, z: 4, core: 2. Of those that a mesh axis runs over, the one named last changes fastest.
Arguments:
- hidden: bfloat16 [8192, 4096], P('seq', 'mp')
- picked: int32 [1024], P('seq'), may hold values from 0 to 8191, as said below
- target: int32 [8192], P('seq'), may hold values from -1 to 1023, as said below
- norm_gain: bfloat16 [4096], replicated, may hold values from 0.099609375 to 1.8984375
- router_weight: bfloat16 [4096], replicated, may hold values from -0.1875 to 0.1875
- w_query: bfloat16 [4096, 2048], P('seq', 'mp')
- w_key: bfloat16 [4096, 2048], P('seq', 'mp')
- w_value: bfloat16 [4096, 2048], P('seq', 'mp'), may hold values from -0.1875 to 0.1875
- w_out: bfloat16 [2048, 4096], P(None, 'mp'), may hold values from -0.125 to 0.125
Outputs:
- mixed: bfloat16 [8192, 4096], P('seq', 'mp')
Inputs may be any that keep to these rules, and one draw needn't show every extreme that they name: `picked`: entry g holds the position of the routed token of rank (g mod 128) * 8 + g div 128, ranks counting the 1024 routed positions in increasing order. target[p] = g where picked[g] = p, and -1 where p is not routed; each aligned block of 1024 positions holds at most 256 routed ones, and some block holds exactly 256.
All inputs are finite; a program needn't handle non-finite values.
Results may differ from a plain program's by a relative error of at most 0.004.
Values may be sent and summed in bfloat16 or wider, within the bound.
A program may use at most 128 MiB of HBM per device.

v0:
```python
import math

import jax
import jax.numpy as jnp
from jax import lax
from jax.sharding import PartitionSpec as P

HEAD_DIM = 128


def rotate(vec, positions):
    half = vec.shape[-1] // 2
    freq = jnp.exp(-math.log(10000.0) * (2.0 * jnp.arange(half, dtype=jnp.float32) / vec.shape[-1]))
    angle = positions.astype(jnp.float32)[:, None] * freq[None, :]
    cosine = jnp.cos(angle)[:, None, :]
    sine = jnp.sin(angle)[:, None, :]
    first = vec[..., :half]
    second = vec[..., half:]
    return jnp.concatenate(
        [first * cosine - second * sine, second * cosine + first * sine], axis=-1
    )


def per_device(hidden, picked, target, norm_gain, router_weight, w_query, w_key, w_value, w_out):
    shards = lax.axis_size("seq")
    here = lax.axis_index("seq")
    tok_rows = hidden.shape[0]
    part_width = hidden.shape[1]
    sel_rows = picked.shape[0]
    bucket = (2 * sel_rows + shards - 1) // shards
    live = target >= 0
    dest = jnp.where(live, target // sel_rows, shards)
    cell = dest * bucket + jnp.where(live, target % sel_rows, 0) % bucket
    table = jnp.full((shards * bucket,), tok_rows, jnp.int32)
    table = table.at[cell].set(jnp.arange(tok_rows, dtype=jnp.int32), mode="drop")
    padded = jnp.concatenate([hidden, jnp.zeros((1, part_width), hidden.dtype)], axis=0)
    outgoing = padded[table].reshape(shards, bucket, part_width)
    slots = jnp.arange(sel_rows, dtype=jnp.int32)
    source = picked // tok_rows
    fetch = source * bucket + slots % bucket
    arrived = lax.all_to_all(outgoing, "seq", split_axis=0, concat_axis=0, tiled=True)
    own_rows = arrived.reshape(shards * bucket, part_width)[fetch]
    full_rows = lax.all_gather(own_rows, "mp", axis=1, tiled=True)
    whole = full_rows.astype(jnp.float32)
    inverse = lax.rsqrt(jnp.mean(whole * whole, axis=-1, keepdims=True) + 1e-05)
    normed = (whole * inverse * norm_gain.astype(jnp.float32)).astype(jnp.bfloat16)
    gate = jax.nn.sigmoid(jnp.dot(full_rows, router_weight, preferred_element_type=jnp.float32))

    def add_rows(piece):
        return jnp.dot(normed, piece, preferred_element_type=jnp.float32)

    query_raw = add_rows(lax.all_gather(w_query, "seq", axis=0, tiled=True))
    key_raw = add_rows(lax.all_gather(w_key, "seq", axis=0, tiled=True))
    value_raw = add_rows(lax.all_gather(w_value, "seq", axis=0, tiled=True))
    heads = w_query.shape[1] // HEAD_DIM
    query = rotate(query_raw.reshape(sel_rows, heads, HEAD_DIM), picked).astype(jnp.bfloat16)
    keys = rotate(key_raw.reshape(sel_rows, heads, HEAD_DIM), picked).astype(jnp.bfloat16)
    values = value_raw.reshape(sel_rows, heads, HEAD_DIM).astype(jnp.bfloat16)
    rank_q = slots * shards + here
    scale = 1.0 / math.sqrt(HEAD_DIM)
    top = jnp.full((heads, sel_rows), -1e30, jnp.float32)
    piece_k = lax.all_gather(keys, "seq", axis=0, tiled=True)
    piece_v = lax.all_gather(values, "seq", axis=0, tiled=True)
    index = jnp.arange(piece_k.shape[0], dtype=jnp.int32)
    rank_k = index % sel_rows * shards + index // sel_rows
    allowed = (rank_k[None, :] <= rank_q[:, None])[None]
    scores = jnp.einsum("qhd,khd->hqk", query, piece_k, preferred_element_type=jnp.float32) * scale
    scores = jnp.where(allowed, scores, -1e30)
    newtop = jnp.maximum(top, jnp.max(scores, axis=-1))
    weights = jnp.where(allowed, jnp.exp(scores - newtop[..., None]), 0.0)
    total = jnp.sum(weights, axis=-1)
    summed = jnp.einsum(
        "hqk,khd->hqd", weights.astype(jnp.bfloat16), piece_v, preferred_element_type=jnp.float32
    )
    top, total, summed = (newtop, total, summed)
    attended = (
        jnp.transpose(summed / total[..., None], (1, 0, 2))
        .reshape(sel_rows, heads * HEAD_DIM)
        .astype(jnp.bfloat16)
    )
    update = jnp.dot(
        lax.all_gather(attended, "mp", axis=1, tiled=True),
        w_out,
        preferred_element_type=jnp.float32,
    )
    new_rows = (own_rows.astype(jnp.float32) + gate[:, None] * update).astype(jnp.bfloat16)
    backward = jnp.zeros((shards * bucket, part_width), jnp.bfloat16).at[fetch].set(new_rows)
    returned = lax.all_to_all(
        backward.reshape(shards, bucket, part_width), "seq", split_axis=0, concat_axis=0, tiled=True
    )
    taken = returned.reshape(shards * bucket, part_width)[jnp.where(live, cell, 0)]
    return jnp.where(live[:, None], taken, hidden)


def solution(mesh):
    placed = (
        P("seq", "mp"),
        P("seq"),
        P("seq"),
        P(),
        P(),
        P("seq", "mp"),
        P("seq", "mp"),
        P("seq", "mp"),
        P(None, "mp"),
    )
    return jax.shard_map(
        per_device, mesh=mesh, in_specs=placed, out_specs=P("seq", "mp"), check_vma=False
    )
```

profile of v0, /device:TPU:31, one launch (start us, length us, event | category | flops | bytes accessed | tf_op | source)
XLA Modules:
  0.0 398.2 jit_solution(2905719914178391769)
XLA Ops:
  6.5 0.7 fusion.40
  7.3 4.3 %scatter_custom_fusion = s32[256]{0:T(256)S(1)} fusion(s32[1024]{0:T(1024)S(1)} %compare_select_fusion.1, s32[1024]{0:T(1024)S(1)} %iota.22, s32[]{:T(128)} %constant.109.clone.1), kind=kCustom, calls=%fused_computation.94 | custom fusion | bytes 1028 | tf_op jit(solution)/shard_map/scatter | solution.py:35
  11.6 1.8 concatenate.11
  13.4 2.0 gather_fusion
  15.3 5.4 %all-to-all-start = ((bf16[8,32,1024]{2,1,0:T(8,128)(2,1)}), bf16[8,32,1024]{2,1,0:T(8,128)(2,1)S(1)}, u32[]{:S(2)}, u32[]{:S(2)}) async-start(bf16[8,32,1024]{2,1,0:T(8,128)(2,1)} %bitcast), calls=%async_computation | async-start | bytes 1048576 | tf_op jit(solution)/shard_map/all_to_all | solution.py:41
  20.8 12.8 %all-to-all-done = bf16[8,32,1024]{2,1,0:T(8,128)(2,1)S(1)} async-done(((bf16[8,32,1024]{2,1,0:T(8,128)(2,1)}), bf16[8,32,1024]{2,1,0:T(8,128)(2,1)S(1)}, u32[]{:S(2)}, u32[]{:S(2)}) %all-to-all-start) | async-done | bytes 524320 | tf_op jit(solution)/shard_map/all_to_all | solution.py:41
  33.6 1.6 gather_fusion.1
  35.3 0.7 all-gather.8.cloned.1.call-update
  36.0 0.7 all-gather.10.cloned.1.call-update
  36.8 0.5 all-gather.14.cloned.1.call-update
  37.7 14.6 %all-gather.18.cloned.1.call-done = bf16[128,4096]{1,0:T(8,128)(2,1)} async-done(((bf16[128,1024]{1,0:T(8,128)(2,1)}), bf16[128,4096]{1,0:T(8,128)(2,1)}) %all-gather.18.cloned.1.call-update) | async-done | bytes 1048592 | tf_op jit(solution)/shard_map/all_gather | solution.py:43
  52.3 1.5 fusion
  53.9 72.0 %all-gather.8.cloned.1.call-done = bf16[4096,512]{1,0:T(8,128)(2,1)} async-done(((bf16[512,512]{1,0:T(8,128)(2,1)}), bf16[4096,512]{1,0:T(8,128)(2,1)}) %all-gather.8.cloned.1.call-update) | async-done | bytes 4194320 | tf_op jit(solution)/shard_map/all_gather | solution.py:52
  125.9 3.3 fusion.53
  129.3 70.5 %all-gather.10.cloned.1.call-done = bf16[4096,512]{1,0:T(8,128)(2,1)} async-done(((bf16[512,512]{1,0:T(8,128)(2,1)}), bf16[4096,512]{1,0:T(8,128)(2,1)}) %all-gather.10.cloned.1.call-update) | async-done | bytes 4194320 | tf_op jit(solution)/shard_map/all_gather | solution.py:53
  199.7 3.0 fusion.51
  203.3 0.8 pad_maximum_fusion
  204.2 69.2 %all-gather.14.cloned.1.call-done = bf16[4096,512]{1,0:T(8,128)(2,1)} async-done(((bf16[512,512]{1,0:T(8,128)(2,1)}), bf16[4096,512]{1,0:T(8,128)(2,1)}) %all-gather.14.cloned.1.call-update) | async-done | bytes 4194320 | tf_op jit(solution)/shard_map/all_gather | solution.py:54
  273.4 3.0 convolution_convert_fusion
  276.4 0.8 copy.15
  277.4 0.4 fusion.13
  277.8 34.7 %all-gather.12.cloned.1.call-done = bf16[1024,4,128]{2,0,1:T(8,128)(2,1)} async-done(((bf16[128,4,128]{2,0,1:T(8,128)(2,1)}), bf16[1024,4,128]{2,0,1:T(8,128)(2,1)}) %all-gather.12.cloned.1.call-update) | async-done | bytes 1048592 | tf_op jit(solution)/shard_map/all_gather | solution.py:62
  312.5 1.9 fusion.3
  314.4 0.7 fusion.4
  315.1 38.3 %all-gather.16.cloned.1.call-done = bf16[1024,4,128]{0,2,1:T(8,128)(2,1)} async-done(((bf16[128,4,128]{0,2,1:T(8,128)(2,1)}), bf16[1024,4,128]{0,2,1:T(8,128)(2,1)}) %all-gather.16.cloned.1.call-update) | async-done | bytes 1048592 | tf_op jit(solution)/shard_map/all_gather | solution.py:63
  353.3 2.2 fusion.9
  355.5 8.3 %all_gather.27 = bf16[128,2048]{0,1:T(8,128)(2,1)S(1)} all-gather(bf16[128,512]{0,1:T(8,128)(2,1)S(1)} %bitcast.36), channel_id=1, replica_groups=mesh['seq'=8,'mp'=4] {'mp'}, dimensions={1}, use_global_device_ids=true | all-gather | bytes 655360 | tf_op jit(solution)/shard_map/all_gather | solution.py:82
  363.9 0.8 fusion.7
  364.6 1.3 scatter_custom_fusion.1
  365.9 18.0 %all_to_all.10 = bf16[8,32,1024]{2,1,0:T(8,128)(2,1)S(1)} all-to-all(bf16[8,32,1024]{2,1,0:T(8,128)(2,1)S(1)} %bitcast.34), channel_id=1, replica_groups=mesh['seq'=8,'mp'=4] {'seq'}, dimensions={0} | all-to-all | bytes 1048576 | tf_op jit(solution)/shard_map/all_to_all | solution.py:88
  383.9 4.1 %gather_fusion.2 = bf16[1024,1024]{1,0:T(8,128)(2,1)S(1)} fusion(bf16[256,1024]{1,0:T(8,128)(2,1)S(1)} %bitcast.32, s32[1024]{0:T(1024)S(1)} %get-tuple-element.5), kind=kCustom, calls=%fused_computation.2 | custom fusion | bytes 4198400 | tf_op jit(solution)/shard_map/gather | solution.py:91
  388.0 3.3 broadcast_select_fusion
  (40 shorter events, 1.5 us)
Async XLA Ops:
  13.4 7.4 %copy-start.5 = (s32[128]{0:T(128)S(1)}, s32[128]{0:T(128)}, u32[]{:S(2)}) copy-start(s32[128]{0:T(128)} %param.10) | copy-start | bytes 1540
  15.3 18.3 %all-to-all-start = ((bf16[8,32,1024]{2,1,0:T(8,128)(2,1)}), bf16[8,32,1024]{2,1,0:T(8,128)(2,1)S(1)}, u32[]{:S(2)}, u32[]{:S(2)}) async-start(bf16[8,32,1024]{2,1,0:T(8,128)(2,1)} %bitcast), calls=%async_computation | async-start | bytes 1048576 | tf_op jit(solution)/shard_map/all_to_all | solution.py:41
  20.8 31.5 %all-gather.18.cloned.1.call-start = ((), (), s32[]{:S(2)}) async-start(), calls=%async_computation.7 | async-start | bytes 1310720 | tf_op jit(solution)/shard_map/all_gather | solution.py:43
  33.6 3.7 copy-start.3
  35.2 90.7 %all-gather.8.cloned.1.call-start = ((), (), s32[]{:S(2)}) async-start(), calls=%async_computation.2 | async-start | bytes 4718592 | tf_op jit(solution)/shard_map/all_gather | solution.py:52
  36.0 163.7 %all-gather.10.cloned.1.call-start = ((), (), s32[]{:S(2)}) async-start(), calls=%async_computation.3 | async-start | bytes 4718592 | tf_op jit(solution)/shard_map/all_gather | solution.py:53
  36.7 236.7 %all-gather.14.cloned.1.call-start = ((), (), s32[]{:S(2)}) async-start(), calls=%async_computation.5 | async-start | bytes 4718592 | tf_op jit(solution)/shard_map/all_gather | solution.py:54
  37.3 275.2 %all-gather.12.cloned.1.call-start = ((), (), s32[]{:S(2)}) async-start(), calls=%async_computation.4 | async-start | bytes 1179648 | tf_op jit(solution)/shard_map/all_gather | solution.py:62
  53.9 145.9 %copy-start.1 = (bf16[128,4096]{1,0:T(8,128)(2,1)S(1)}, bf16[128,4096]{1,0:T(8,128)(2,1)}, u32[]{:S(2)}) copy-start(bf16[128,4096]{1,0:T(8,128)(2,1)} %all-gather.18.cloned.1.call-done) | copy-start | bytes 3145732
  204.1 73.1 %copy-start.4 = (bf16[4096]{0:T(1024)(128)(2,1)S(1)}, bf16[4096]{0:T(1024)(128)(2,1)}, u32[]{:S(2)}) copy-start(bf16[4096]{0:T(1024)(128)(2,1)} %param.13) | copy-start | bytes 24580
  204.1 149.2 %all-gather.16.cloned.1.call-start = ((), (), s32[]{:S(2)}) async-start(), calls=%async_computation.6 | async-start | bytes 1179648 | tf_op jit(solution)/shard_map/all_gather | solution.py:63
  353.3 10.5 %copy-start = (bf16[2048,1024]{1,0:T(8,128)(2,1)S(1)}, bf16[2048,1024]{1,0:T(8,128)(2,1)}, u32[]{:S(2)}) copy-start(bf16[2048,1024]{1,0:T(8,128)(2,1)} %param.17) | copy-start | bytes 12582916
  353.3 10.5 %copy-start.2 = (bf16[128,1024]{1,0:T(8,128)(2,1)S(1)}, bf16[128,1024]{1,0:T(8,128)(2,1)}, u32[]{:S(2)}) copy-start(bf16[128,1024]{1,0:T(8,128)(2,1)} %gather_fusion.1) | copy-start | bytes 786436
Sparse Core Ops, SparseCore 0:
  35.4 16.9 all-gather.17
  54.5 71.3 all-gather.7
  128.0 71.6 all-gather.9
  201.7 71.6 all-gather.13
  275.4 36.9 all-gather.11
  314.4 38.9 all-gather.15
where the time goes:
time: 403 us; the launch traced here: 398 us
  waiting for transfers between devices  314 us (78%)
  blocking collectives  26.3 us (7%)
  local copies, waits for them, and re-layouts  16.3 us (4%)
  matrix products  14.5 us (4%)
  between operations  13.7 us (3%)
  other arithmetic  7.68 us (2%)
  starting transfers between devices  5.64 us (1%)
    all_gather x1, waiting for transfers between devices, per_device(): query_raw = add_rows(lax.all_gather(w_query, 'seq', axis=0, tiled=True))  72 us
    all_gather x1, waiting for transfers between devices, per_device(): key_raw = add_rows(lax.all_gather(w_key, 'seq', axis=0, tiled=True))  70.5 us
    all_gather x1, waiting for transfers between devices, per_device(): value_raw = add_rows(lax.all_gather(w_value, 'seq', axis=0, tiled=True))  69.2 us
    all_gather x1, waiting for transfers between devices, per_device(): piece_v = lax.all_gather(values, 'seq', axis=0, tiled=True)  38.3 us
    all_gather x1, waiting for transfers between devices, per_device(): piece_k = lax.all_gather(keys, 'seq', axis=0, tiled=True)  34.7 us
    all_to_all x1, blocking collectives, per_device(): lax.all_to_all(backward.reshape(shards, bucket, part_width), 'seq', split...  18 us
    all_gather x1, waiting for transfers between devices, per_device(): full_rows = lax.all_gather(own_rows, 'mp', axis=1, tiled=True)  14.6 us
    all_to_all x1, waiting for transfers between devices, per_device(): lax.all_to_all(outgoing, 'seq', split_axis=0, concat_axis=0, tiled=True)  12.8 us
  transfers between devices with their start and end apart: 7, of which 7 were waited for; matrix products, arithmetic and copies ran while one was open for 4% of the time, Pallas kernels for 0%

commit v1 on v0

--- a/solution.py
+++ b/solution.py
@@ -3,9 +3,14 @@
 import jax
 import jax.numpy as jnp
 from jax import lax
+from jax.experimental import pallas as pl
+from jax.experimental.pallas import tpu as pltpu
 from jax.sharding import PartitionSpec as P
 
 HEAD_DIM = 128
+MESH = pl.DeviceIdType.MESH
+BF = jnp.bfloat16
+F32 = jnp.float32
 
 
 def rotate(vec, positions):
@@ -21,7 +26,7 @@
     )
 
 
-def per_device(hidden, picked, target, norm_gain, router_weight, w_query, w_key, w_value, w_out):
+def general(hidden, picked, target, norm_gain, router_weight, w_query, w_key, w_value, w_out):
     shards = lax.axis_size("seq")
     here = lax.axis_index("seq")
     tok_rows = hidden.shape[0]
@@ -92,6 +97,353 @@
     return jnp.where(live[:, None], taken, hidden)
 
 
+def slots_of(target, half):
+    live = target >= 0
+    rank = (target % 128) * 8 + target // 128
+    first = jnp.min(jnp.where(live, rank, 1 << 20), axis=1, keepdims=True)
+    parity = rank % 2
+    index = rank // 2
+    slot = parity * half + index - (first - parity + 1) // 2
+    return jnp.where(live, slot, -1), index
+
+
+def one_hot(row, count):
+    return (lax.broadcasted_iota(jnp.int32, (count, row.shape[1]), 0) == row).astype(BF)
+
+
+def mix_kernel(
+    target_ref, hidden_ref, gain_ref, router_ref, wq_ref, wk_ref, wv_ref,
+    rows_out, gate_out, att_out,
+    stats, nsend, aux, xbuf, auxbuf, pick, dense, ysend, yrecv, zsend, zown, zrecv,
+    qbuf, kbuf, vbuf, att, msg, arecv, cosine, sine,
+    st_send, st_recv, x_send, x_recv, a_send, a_recv, fx_send, fa_send,
+    y_send, y_recv, z_send, z_recv, kv_send, kv_recv, m_send, m_recv,
+):
+    s = lax.axis_index("seq")
+    m = lax.axis_index("mp")
+    z, y = s // 2, s % 2
+    x, c = m // 2, m % 2
+    me = s * 4 + m
+    weights = (wk_ref, wv_ref, wq_ref)
+
+    def at(seq, mp):
+        return {"seq": seq, "mp": mp}
+
+    def remote(src, dst, send, recv, seq, mp):
+        return pltpu.make_async_remote_copy(
+            src_ref=src, dst_ref=dst, send_sem=send, recv_sem=recv,
+            device_id=at(seq, mp), device_id_type=MESH,
+        )
+
+    barrier = pltpu.get_barrier_semaphore()
+
+    @pl.loop(1, 32)
+    def _(step):
+        other = lax.rem(me + step, 32)
+        pl.semaphore_signal(barrier, inc=1, device_id=at(other // 4, other % 4), device_id_type=MESH)
+
+    slot, index = slots_of(target_ref[...], 128)
+    chosen = one_hot(slot, 256)
+    rows = jnp.dot(chosen, hidden_ref[...], preferred_element_type=F32)
+    rows_out[...] = rows.astype(BF)
+    squares = jnp.sum(rows * rows, axis=1, keepdims=True)
+    logit = jnp.sum(rows * router_ref[pl.ds(m, 1), :], axis=1, keepdims=True)
+    lane = lax.broadcasted_iota(jnp.int32, (256, 128), 1)
+    table = jnp.where(lane == 0, squares, jnp.where(lane == 1, logit, 0.0))
+    stats[m] = table.T[0:8]
+    sub = lax.broadcasted_iota(jnp.int32, (8, 1024), 0)
+    place = lax.broadcasted_iota(jnp.int32, (8, 1024), 1)
+    parts = jnp.where(sub == 0, index // 16, jnp.where(sub == 1, index % 16, jnp.where(
+        sub == 2, place // 32, jnp.where(sub == 3, place % 32, 1))))
+    parts = lax.dot_general(
+        parts.astype(F32).astype(BF), chosen, (((1,), (1,)), ((), ())), preferred_element_type=F32)
+    mine = jnp.where(parts[4:5] > 0.5, parts[0:1] * 16.0 + parts[1:2], -1.0)
+    spot = parts[2:3] * 32.0 + parts[3:4] + (s * 1024).astype(F32)
+    aux[...] = jnp.where(lax.broadcasted_iota(jnp.int32, (8, 256), 0) == 0, mine, spot)
+
+    pl.semaphore_wait(barrier, 31)
+    for step in range(1, 4):
+        other = lax.rem(m + step, 4)
+        remote(stats.at[m], stats.at[m], st_send.at[step - 1], st_recv.at[m], s, other).start()
+    for step in range(1, 4):
+        other = lax.rem(m + step, 4)
+        copy = remote(stats.at[other], stats.at[other], st_send.at[step - 1], st_recv.at[other], s, other)
+        copy.wait_recv()
+    total = stats[0] + stats[1] + stats[2] + stats[3]
+    total = jnp.concatenate([total] * 16, axis=0).T
+    gate_out[...] = jnp.broadcast_to(1.0 / (1.0 + jnp.exp(-total[:, 1:2])), (256, 128))
+    inverse = lax.rsqrt(total[:, 0:1] * (1.0 / 4096) + 1e-05)
+    normed = (rows * inverse * gain_ref[pl.ds(m, 1), :]).astype(BF)
+    for half in range(2):
+        nsend[half] = normed[:, half * 512:half * 512 + 512].reshape(2, 128, 512)
+
+    here = pl.ds(pl.multiple_of(s * 128, 128), 128)
+    for half in range(2):
+        for across in range(2):
+            number = half * 2 + across
+            seq, mp = 2 * m + half, c + 2 * across
+            own = jnp.logical_and(seq == s, mp == m)
+
+            @pl.when(own)
+            def _():
+                xbuf[:, here, :] = nsend[half]
+                auxbuf[s] = aux[...]
+
+            @pl.when(jnp.logical_not(own))
+            def _():
+                remote(nsend.at[half], xbuf.at[:, here, :], x_send.at[number], x_recv.at[s], seq, mp).start()
+                remote(aux, auxbuf.at[s], a_send.at[number], a_recv.at[s], seq, mp).start()
+
+    direct = c == z % 2
+    sibling = m + 1 - 2 * c
+
+    @pl.loop(0, 8)
+    def _(step):
+        block = lax.rem(s + step, 8)
+        there = pl.ds(pl.multiple_of(block * 128, 128), 128)
+        pair = (
+            remote(xbuf.at[:, there, :], xbuf.at[:, there, :], fx_send.at[block], x_recv.at[block], s, sibling),
+            remote(auxbuf.at[block], auxbuf.at[block], fa_send.at[block], a_recv.at[block], s, sibling),
+        )
+
+        @pl.when(jnp.logical_not(jnp.logical_and(m == z, block == s)))
+        def _():
+            for copy in pair:
+                copy.wait_recv()
+
+        @pl.when(direct)
+        def _():
+            for copy in pair:
+                copy.start()
+
+    for parity in range(2):
+        line = jnp.concatenate(
+            [auxbuf[b][0:1, parity * 128:parity * 128 + 128] for b in range(8)], axis=1).astype(jnp.int32)
+
+        @pl.loop(0, 4)
+        def _(tile):
+            rows_here = pl.ds(pl.multiple_of(tile * 128, 128), 128)
+            hot = (lax.broadcasted_iota(jnp.int32, (128, 1024), 0) + tile * 128 == line).astype(BF)
+            pick[parity, rows_here, :] = hot
+            dense[parity, rows_here, :] = jnp.dot(
+                hot, xbuf[parity], preferred_element_type=F32).astype(BF)
+
+    other_y = 1 - y
+    near = s + 1 - 2 * y
+
+    def ycopy(kind):
+        return remote(ysend.at[kind], yrecv.at[kind], y_send.at[kind], y_recv.at[kind], near, m)
+
+    def zcopy(kind, step):
+        peer = lax.rem(z + step, 4)
+        return remote(zsend.at[kind, peer], zrecv.at[kind, z], z_send.at[kind, peer], z_recv.at[kind, z], 2 * peer + y, m)
+
+    def zwait(kind, step):
+        peer = lax.rem(z + step, 4)
+        remote(zsend.at[kind, peer], zrecv.at[kind, peer], z_send.at[kind, peer], z_recv.at[kind, peer], 2 * peer + y, m).wait_recv()
+
+    for kind in range(3):
+        @pl.loop(0, 2)
+        def _(tile):
+            part = pl.ds(pl.multiple_of(tile * 256, 256), 256)
+            ysend[kind, part, :] = jnp.dot(
+                dense[other_y, part, :], weights[kind][...], preferred_element_type=F32).astype(BF)
+
+        ycopy(kind).start()
+
+    places = jnp.concatenate([
+        jnp.where(y == 0, auxbuf[b][1:2, 0:128], auxbuf[b][1:2, 128:256]) for b in range(8)], axis=1)
+    lanes = lax.broadcasted_iota(jnp.int32, (1, 128), 1) % 64
+    freq = jnp.exp(-math.log(10000.0) * (2.0 * lanes.astype(F32) / 128))
+    sign = jnp.where(lax.broadcasted_iota(jnp.int32, (1, 128), 1) < 64, -1.0, 1.0)
+
+    @pl.loop(0, 4)
+    def _(tile):
+        part = pl.ds(pl.multiple_of(tile * 128, 128), 128)
+        where = jnp.sum(pick[y, part, :].astype(F32) * places, axis=1, keepdims=True)
+        angle = where * freq
+        cosine[part, :] = jnp.cos(angle)
+        sine[part, :] = jnp.sin(angle) * sign
+
+    for kind in range(3):
+        ycopy(kind).wait_recv()
+
+        @pl.loop(0, 2)
+        def _(tile):
+            part = pl.ds(pl.multiple_of(tile * 256, 256), 256)
+            value = jnp.dot(dense[y, part, :], weights[kind][...], preferred_element_type=F32)
+            value = value + yrecv[kind, part, :].astype(F32)
+            for head in range(4):
+                zsend[kind, head, part, :] = value[:, head * 128:head * 128 + 128].astype(BF)
+
+        for step in range(1, 4):
+            zcopy(kind, step).start()
+
+    def kvcopy(buf, kind):
+        return remote(buf.at[y], buf.at[y], kv_send.at[kind], kv_recv.at[kind], near, m)
+
+    for kind in range(3):
+        for step in range(1, 4):
+            zwait(kind, step)
+        value = zsend[kind, z].astype(F32)
+        for step in range(1, 4):
+            value = value + zrecv[kind, lax.rem(z + step, 4)].astype(F32)
+        if kind != 1:
+            value = value * cosine[...] + pltpu.roll(value, 64, 1) * sine[...]
+        if kind == 2:
+            qbuf[...] = value.astype(BF)
+        else:
+            buf = (kbuf, vbuf)[kind]
+            buf[y] = value.astype(BF)
+            kvcopy(buf, kind).start()
+    for kind, buf in enumerate((kbuf, vbuf)):
+        remote(buf.at[other_y], buf.at[other_y], kv_send.at[kind], kv_recv.at[kind], near, m).wait_recv()
+
+    @pl.loop(0, 4)
+    def _(tile):
+        part = pl.ds(pl.multiple_of(tile * 128, 128), 128)
+        keys = kbuf[...].reshape(1024, 128)
+        scores = lax.dot_general(
+            qbuf[part, :], keys, (((1,), (1,)), ((), ())), preferred_element_type=F32) * (1.0 / math.sqrt(HEAD_DIM))
+        column = lax.broadcasted_iota(jnp.int32, (128, 1024), 1)
+        rank_k = 2 * (column % 512) + column // 512
+        rank_q = 2 * (lax.broadcasted_iota(jnp.int32, (128, 1024), 0) + tile * 128) + y
+        allowed = rank_k <= rank_q
+        scores = jnp.where(allowed, scores, -1e30)
+        top = jnp.max(scores, axis=1, keepdims=True)
+        weight = jnp.where(allowed, jnp.exp(scores - top), 0.0)
+        total = jnp.sum(weight, axis=1, keepdims=True)
+        summed = jnp.dot(weight.astype(BF), vbuf[...].reshape(1024, 128), preferred_element_type=F32)
+        att[part, :] = (summed / total).astype(BF)
+
+    messages = lax.dot_general(
+        pick[y], att[...], (((0,), (0,)), ((), ())), preferred_element_type=F32)
+    msg[...] = messages.astype(BF).reshape(8, 128, 128)
+    part = pl.ds(pl.multiple_of(y * 128, 128), 128)
+    head = m * 4 + z
+    column = pl.ds(pl.multiple_of(head * 128, 128), 128)
+    arecv[part, column] = msg[s]
+
+    def mcopy(step):
+        other = lax.rem(me + step, 32)
+        return remote(msg.at[other // 4], arecv.at[part, column], m_send.at[other], m_recv.at[me], other // 4, other % 4)
+
+    @pl.loop(1, 32)
+    def _(step):
+        mcopy(step).start()
+
+    @pl.loop(1, 32)
+    def _(step):
+        other = lax.rem(me + step, 32)
+        seq, mp = other // 4, other % 4
+        to_part = pl.ds(pl.multiple_of(seq % 2 * 128, 128), 128)
+        to_column = pl.ds(pl.multiple_of((mp * 4 + seq // 2) * 128, 128), 128)
+        remote(msg.at[seq], arecv.at[to_part, to_column], m_send.at[other], m_recv.at[other], seq, mp).wait_recv()
+
+    att_out[...] = arecv[...]
+
+    for step in range(1, 4):
+        other = lax.rem(m + step, 4)
+        remote(stats.at[m], stats.at[m], st_send.at[step - 1], st_recv.at[m], s, other).wait_send()
+    for half in range(2):
+        for across in range(2):
+            number = half * 2 + across
+            seq, mp = 2 * m + half, c + 2 * across
+
+            @pl.when(jnp.logical_not(jnp.logical_and(seq == s, mp == m)))
+            def _():
+                remote(nsend.at[half], xbuf.at[:, here, :], x_send.at[number], x_recv.at[s], seq, mp).wait_send()
+                remote(aux, auxbuf.at[s], a_send.at[number], a_recv.at[s], seq, mp).wait_send()
+
+    @pl.when(direct)
+    def _():
+        @pl.loop(0, 8)
+        def _(block):
+            there = pl.ds(pl.multiple_of(block * 128, 128), 128)
+            remote(xbuf.at[:, there, :], xbuf.at[:, there, :], fx_send.at[block], x_recv.at[block], s, sibling).wait_send()
+            remote(auxbuf.at[block], auxbuf.at[block], fa_send.at[block], a_recv.at[block], s, sibling).wait_send()
+
+    for kind in range(3):
+        ycopy(kind).wait_send()
+        for step in range(1, 4):
+            zcopy(kind, step).wait_send()
+    for kind, buf in enumerate((kbuf, vbuf)):
+        kvcopy(buf, kind).wait_send()
+
+    @pl.loop(1, 32)
+    def _(step):
+        mcopy(step).wait_send()
+
+
+def finish_kernel(target_ref, hidden_ref, rows_ref, gate_ref, att_ref, w_out_ref, mixed_ref):
+    slot, _ = slots_of(target_ref[...], 128)
+    chosen = one_hot(slot, 256)
+    flags = lax.dot_general(
+        chosen, jnp.ones((256, 128), BF), (((0,), (0,)), ((), ())), preferred_element_type=F32)
+    update = jnp.dot(att_ref[...], w_out_ref[...], preferred_element_type=F32)
+    fresh = (rows_ref[...].astype(F32) + gate_ref[:, 0:1] * update).astype(BF)
+    spread = lax.dot_general(chosen, fresh, (((0,), (0,)), ((), ())), preferred_element_type=F32)
+    mixed_ref[...] = jnp.where(flags[:, 0:1] > 0.5, spread, hidden_ref[...].astype(F32)).astype(BF)
+
+
+def fused(hidden, picked, target, norm_gain, router_weight, w_query, w_key, w_value, w_out):
+    target = target.reshape(1, 1024)
+    gain = norm_gain.reshape(4, 1024).astype(F32)
+    router = router_weight.reshape(4, 1024).astype(F32)
+    dma = pltpu.SemaphoreType.DMA
+    rows, gate, att = pl.pallas_call(
+        mix_kernel,
+        out_shape=(
+            jax.ShapeDtypeStruct((256, 1024), BF),
+            jax.ShapeDtypeStruct((256, 128), F32),
+            jax.ShapeDtypeStruct((256, 2048), BF),
+        ),
+        in_specs=[pl.BlockSpec(memory_space=pltpu.VMEM)] * 7,
+        out_specs=[pl.BlockSpec(memory_space=pltpu.VMEM)] * 3,
+        scratch_shapes=[
+            pltpu.VMEM((4, 8, 256), F32),
+            pltpu.VMEM((2, 2, 128, 512), BF),
+            pltpu.VMEM((8, 256), F32),
+            pltpu.VMEM((2, 1024, 512), BF),
+            pltpu.VMEM((8, 8, 256), F32),
+            pltpu.VMEM((2, 512, 1024), BF),
+            pltpu.VMEM((2, 512, 512), BF),
+            pltpu.VMEM((3, 512, 512), BF),
+            pltpu.VMEM((3, 512, 512), BF),
+            pltpu.VMEM((3, 4, 512, 128), BF),
+            pltpu.VMEM((8, 128), F32),
+            pltpu.VMEM((3, 4, 512, 128), BF),
+            pltpu.VMEM((512, 128), BF),
+            pltpu.VMEM((2, 512, 128), BF),
+            pltpu.VMEM((2, 512, 128), BF),
+            pltpu.VMEM((512, 128), BF),
+            pltpu.VMEM((8, 128, 128), BF),
+            pltpu.VMEM((256, 2048), BF),
+            pltpu.VMEM((512, 128), F32),
+            pltpu.VMEM((512, 128), F32),
+            dma((3,)), dma((4,)), dma((4,)), dma((8,)), dma((4,)), dma((8,)), dma((8,)), dma((8,)),
+            dma((3,)), dma((3,)), dma((3, 4)), dma((3, 4)), dma((2,)), dma((2,)), dma((32,)), dma((32,)),
+        ],
+        compiler_params=pltpu.CompilerParams(
+            collective_id=0, has_side_effects=True, vmem_limit_bytes=48 * 2 ** 20),
+    )(target, hidden, gain, router, w_query, w_key, w_value)
+    return pl.pallas_call(
+        finish_kernel,
+        out_shape=jax.ShapeDtypeStruct((1024, 1024), BF),
+        in_specs=[pl.BlockSpec(memory_space=pltpu.VMEM)] * 6,
+        out_specs=pl.BlockSpec(memory_space=pltpu.VMEM),
+        compiler_params=pltpu.CompilerParams(vmem_limit_bytes=48 * 2 ** 20),
+    )(target, hidden, rows, gate, att, w_out)
+
+
+def per_device(hidden, picked, target, *rest):
+    small = (
+        lax.axis_size("seq") == 8 and lax.axis_size("mp") == 4
+        and hidden.shape == (1024, 1024) and picked.shape[0] == 128
+    )
+    return (fused if small else general)(hidden, picked, target, *rest)
+
+
 def solution(mesh):
     placed = (
         P("seq", "mp"),

time: 403 us -> 146 us (0.36); the launches traced: 398 us -> 145 us
  waiting for transfers between devices: 314 us -> 0 us
  Pallas kernels: 0 us -> 139 us
  blocking collectives: 26.3 us -> 0 us
  matrix products: 14.5 us -> 0 us
  between operations: 13.7 us -> 0.02 us
  local copies, waits for them, and re-layouts: 16.3 us -> 6.82 us
  other arithmetic: 7.68 us -> 0 us
  starting transfers between devices: 5.64 us -> 0 us
    all_gather x6 -> x0, waiting for transfers between devices: 299 us -> none  [the longest x1 72 us: per_device(): query_raw = add_rows(lax.all_gather(w_query, 'seq', axis=0, tiled=True))]
    pallas_call x0 -> x2, Pallas kernels: none -> 139 us  [the longest x1 133 us: fused(): pl.pallas_call(mix_kernel, out_shape=(jax.ShapeDtypeStruct((256, 1024), B...]
    all_to_all x1 -> x0, blocking collectives: 18 us -> none  [per_device(): lax.all_to_all(backward.reshape(shards, bucket, part_width), 'seq', split...]
    dot_general x7 -> x0, matrix products: 14.5 us -> none  [the longest x3 9.26 us: add_rows(): return jnp.dot(normed, piece, preferred_element_type=jnp.float32)]
    all_to_all x1 -> x0, waiting for transfers between devices: 12.8 us -> none  [per_device(): lax.all_to_all(outgoing, 'seq', split_axis=0, concat_axis=0, tiled=True)]
    all_gather x1 -> x0, blocking collectives: 8.33 us -> none  [per_device(): lax.all_gather(attended, 'mp', axis=1, tiled=True)]
    gather x3 -> x0, local copies, waits for them, and re-layouts: 7.58 us -> none  [the longest x1 4.06 us: per_device(): returned.reshape(shards * bucket, part_width)[jnp.where(live, cell, 0)]]
    scatter x2 -> x0, local copies, waits for them, and re-layouts: 5.61 us -> none  [the longest x1 4.3 us: per_device(): table.at[cell].set(jnp.arange(tok_rows, dtype=jnp.int32), mode='drop')]
  transfers between devices with their start and end apart: 7 -> 0, of which waited for: 7 -> 0; matrix products, arithmetic and copies ran while one was open for 4% -> 0% of each run, Pallas kernels for 0% -> 0%
where the time goes in v1:
time: 146 us; the launch traced here: 145 us
  Pallas kernels  139 us (95%)
  local copies, waits for them, and re-layouts  6.82 us (5%)
    pallas_call x1, Pallas kernels, fused(): pl.pallas_call(mix_kernel, out_shape=(jax.ShapeDtypeStruct((256, 1024), B...  133 us
    pallas_call x1, Pallas kernels, fused(): pl.pallas_call(finish_kernel, out_shape=jax.ShapeDtypeStruct((1024, 1024)...  5.74 us
    unnamed x10, local copies, waits for them, and re-layouts  5.4 us

profile of v1, /device:TPU:31, one launch (start us, length us, event | category | flops | bytes accessed | tf_op | source)
XLA Modules:
  0.0 145.4 jit_solution(16454161242743566822)
XLA Ops:
  0.0 0.7 reshape.10.gain_ref
  0.7 0.7 reshape.11.router_ref
  1.4 0.0 copy-start
  1.4 1.6 %copy-done = bf16[1024,1024]{1,0:T(8,128)(2,1)S(1)} copy-done((bf16[1024,1024]{1,0:T(8,128)(2,1)S(1)}, bf16[1024,1024]{1,0:T(8,128)(2,1)}, u32[]{:S(2)}) %copy-start) | copy-done | bytes 2097176
  3.0 0.0 copy-start.1
  3.0 1.0 copy-done.1
  4.1 0.0 copy-start.2
  4.1 1.0 copy-done.2
  5.1 0.0 copy-start.3
  5.1 1.0 copy-done.3
  6.1 0.0 copy-start.4
  6.1 0.7 copy-done.4
  6.8 132.8 %shard_map.82 = (bf16[256,1024]{1,0:T(8,128)(2,1)S(1)}, f32[256,128]{1,0:T(8,128)S(1)}, bf16[256,2048]{1,0:T(8,128)(2,1)S(1)}) custom-call(s32[1,1024]{1,0:T(1,128)S(1)} %bitcast.1, bf16[1024,1024]{1,0:T(8,128)(2,1)S(1)} %copy-done, f32[4,1024]{1,0:T(4,128)S(1)} %reshape.10.gain_ref, f32[4,1024]{1,0:T(4,128)S(1)} %reshape.11.router_ref, ...), custom_call_target="tpu_custom_call" | custom-call | tf_op jit(solution)/shard_map/pallas_call | solution.py:394
  139.6 5.7 %shard_map.83 = bf16[1024,1024]{1,0:T(8,128)(2,1)} custom-call(s32[1,1024]{1,0:T(1,128)S(1)} %bitcast.2, bf16[1024,1024]{1,0:T(8,128)(2,1)S(1)} %copy-done, bf16[256,1024]{1,0:T(8,128)(2,1)S(1)} %get-tuple-element.8.rows_ref, f32[256,128]{1,0:T(8,128)S(1)} %get-tuple-element.9.gate_ref, bf16[256,2048]{1,0:T(8,128)(2,1)S(1)} %get-tuple-element.10.att_ref, ...), custom_call_target="tpu_custom_call" | custom-call | tf_op jit(solution)/shard_map/pallas_call | solution.py:430
Async XLA Ops:
  1.4 1.6 %copy-start = (bf16[1024,1024]{1,0:T(8,128)(2,1)S(1)}, bf16[1024,1024]{1,0:T(8,128)(2,1)}, u32[]{:S(2)}) copy-start(bf16[1024,1024]{1,0:T(8,128)(2,1)} %hidden_ref.3) | copy-start | bytes 6291460
  3.0 1.0 copy-start.1
  4.1 1.0 copy-start.2
  5.1 1.0 copy-start.3
  6.1 0.7 copy-start.4

commit v2 on v1

--- a/solution.py
+++ b/solution.py
@@ -112,12 +112,13 @@
 
 
 def mix_kernel(
-    target_ref, hidden_ref, gain_ref, router_ref, wq_ref, wk_ref, wv_ref,
+    target_ref, hidden_hbm, gain_ref, router_ref, wq_ref, wk_ref, wv_ref,
     rows_out, gate_out, att_out,
-    stats, nsend, aux, xbuf, auxbuf, pick, dense, ysend, yrecv, zsend, zown, zrecv,
+    hidden_ref, wbuf, stats, nsend, aux, xbuf, auxbuf, pick, dense, zsend, zrecv,
     qbuf, kbuf, vbuf, att, msg, arecv, cosine, sine,
-    st_send, st_recv, x_send, x_recv, a_send, a_recv, fx_send, fa_send,
-    y_send, y_recv, z_send, z_recv, kv_send, kv_recv, m_send, m_recv,
+    h_sem, w_sem, w_send, w_recv,
+    st_send, st_recv, x_send, x_recv, a_send, a_recv, fx_send, fa_send, gx_send, ga_send,
+    z_send, z_recv, kv_send, kv_recv, m_send, m_recv,
 ):
     s = lax.axis_index("seq")
     m = lax.axis_index("mp")
@@ -141,6 +142,24 @@
     def _(step):
         other = lax.rem(me + step, 32)
         pl.semaphore_signal(barrier, inc=1, device_id=at(other // 4, other % 4), device_id_type=MESH)
+
+    near = s + 1 - 2 * y
+    other_y = 1 - y
+    hidden_copy = pltpu.make_async_copy(hidden_hbm, hidden_ref, h_sem)
+    hidden_copy.start()
+
+    def wcopy(kind):
+        return remote(weights[kind], wbuf.at[kind, y], w_send.at[kind], w_recv.at[kind], near, m)
+
+    def wlocal(kind):
+        return pltpu.make_async_copy(weights[kind], wbuf.at[kind, y], w_sem.at[kind])
+
+    pl.semaphore_wait(barrier, 31)
+    for kind in range(3):
+        wcopy(kind).start()
+    for kind in range(3):
+        wlocal(kind).start()
+    hidden_copy.wait()
 
     slot, index = slots_of(target_ref[...], 128)
     chosen = one_hot(slot, 256)
@@ -161,7 +180,6 @@
     spot = parts[2:3] * 32.0 + parts[3:4] + (s * 1024).astype(F32)
     aux[...] = jnp.where(lax.broadcasted_iota(jnp.int32, (8, 256), 0) == 0, mine, spot)
 
-    pl.semaphore_wait(barrier, 31)
     for step in range(1, 4):
         other = lax.rem(m + step, 4)
         remote(stats.at[m], stats.at[m], st_send.at[step - 1], st_recv.at[m], s, other).start()
@@ -173,66 +191,76 @@
     total = jnp.concatenate([total] * 16, axis=0).T
     gate_out[...] = jnp.broadcast_to(1.0 / (1.0 + jnp.exp(-total[:, 1:2])), (256, 128))
     inverse = lax.rsqrt(total[:, 0:1] * (1.0 / 4096) + 1e-05)
-    normed = (rows * inverse * gain_ref[pl.ds(m, 1), :]).astype(BF)
+    nsend[...] = (rows * inverse * gain_ref[pl.ds(m, 1), :]).astype(BF)
+
+    here = pl.ds(pl.multiple_of(s * 128, 128), 128)
+
+    def xcopies(half):
+        seq, mp = 2 * m + half, c + 2 * lax.rem(y + half, 2)
+        own = jnp.logical_and(seq == s, mp == m)
+        return own, (
+            remote(nsend.at[pl.ds(half * 128, 128), :], xbuf.at[here, :], x_send.at[half], x_recv.at[s], seq, mp),
+            remote(aux, auxbuf.at[s], a_send.at[half], a_recv.at[s], seq, mp),
+        )
+
     for half in range(2):
-        nsend[half] = normed[:, half * 512:half * 512 + 512].reshape(2, 128, 512)
-
-    here = pl.ds(pl.multiple_of(s * 128, 128), 128)
-    for half in range(2):
-        for across in range(2):
-            number = half * 2 + across
-            seq, mp = 2 * m + half, c + 2 * across
-            own = jnp.logical_and(seq == s, mp == m)
-
-            @pl.when(own)
-            def _():
-                xbuf[:, here, :] = nsend[half]
-                auxbuf[s] = aux[...]
-
-            @pl.when(jnp.logical_not(own))
-            def _():
-                remote(nsend.at[half], xbuf.at[:, here, :], x_send.at[number], x_recv.at[s], seq, mp).start()
-                remote(aux, auxbuf.at[s], a_send.at[number], a_recv.at[s], seq, mp).start()
+        own, pair = xcopies(half)
+
+        @pl.when(own)
+        def _():
+            xbuf[here, :] = nsend[half * 128:half * 128 + 128, :]
+            auxbuf[s] = aux[...]
+
+        @pl.when(jnp.logical_not(own))
+        def _():
+            for copy in pair:
+                copy.start()
 
     direct = c == z % 2
-    sibling = m + 1 - 2 * c
+
+    def forward(step, to_core):
+        landing = lax.rem(x + y + step // 4, 2)
+        block = 2 * lax.rem(z + step, 4) + landing
+        there = pl.ds(pl.multiple_of(block * 128, 128), 128)
+        mp = m + 1 - 2 * c if to_core else lax.rem(m + 2, 4)
+        x_sems, a_sems = (fx_send, fa_send) if to_core else (gx_send, ga_send)
+        return block, (
+            remote(xbuf.at[there, :], xbuf.at[there, :], x_sems.at[block], x_recv.at[block], s, mp),
+            remote(auxbuf.at[block], auxbuf.at[block], a_sems.at[block], a_recv.at[block], s, mp),
+        )
 
     @pl.loop(0, 8)
     def _(step):
-        block = lax.rem(s + step, 8)
-        there = pl.ds(pl.multiple_of(block * 128, 128), 128)
-        pair = (
-            remote(xbuf.at[:, there, :], xbuf.at[:, there, :], fx_send.at[block], x_recv.at[block], s, sibling),
-            remote(auxbuf.at[block], auxbuf.at[block], fa_send.at[block], a_recv.at[block], s, sibling),
-        )
-
-        @pl.when(jnp.logical_not(jnp.logical_and(m == z, block == s)))
+        block, pair = forward(step, True)
+        _, across = forward(step, False)
+
+        @pl.when(jnp.logical_not(jnp.logical_and(jnp.logical_and(m == z, x == 0), block == s)))
         def _():
             for copy in pair:
                 copy.wait_recv()
 
+        @pl.when(jnp.logical_and(direct, step < 4))
+        def _():
+            for copy in across:
+                copy.start()
+
         @pl.when(direct)
         def _():
             for copy in pair:
                 copy.start()
 
-    for parity in range(2):
-        line = jnp.concatenate(
-            [auxbuf[b][0:1, parity * 128:parity * 128 + 128] for b in range(8)], axis=1).astype(jnp.int32)
-
-        @pl.loop(0, 4)
-        def _(tile):
-            rows_here = pl.ds(pl.multiple_of(tile * 128, 128), 128)
-            hot = (lax.broadcasted_iota(jnp.int32, (128, 1024), 0) + tile * 128 == line).astype(BF)
-            pick[parity, rows_here, :] = hot
-            dense[parity, rows_here, :] = jnp.dot(
-                hot, xbuf[parity], preferred_element_type=F32).astype(BF)
-
-    other_y = 1 - y
-    near = s + 1 - 2 * y
-
-    def ycopy(kind):
-        return remote(ysend.at[kind], yrecv.at[kind], y_send.at[kind], y_recv.at[kind], near, m)
+    def line_of(which):
+        return jnp.concatenate([jnp.where(
+            y == 0, auxbuf[b][which:which + 1, 0:128], auxbuf[b][which:which + 1, 128:256]) for b in range(8)], axis=1)
+
+    line = line_of(0).astype(jnp.int32)
+
+    @pl.loop(0, 4)
+    def _(tile):
+        part = pl.ds(pl.multiple_of(tile * 128, 128), 128)
+        hot = (lax.broadcasted_iota(jnp.int32, (128, 1024), 0) + tile * 128 == line).astype(BF)
+        pick[part, :] = hot
+        dense[part, :] = jnp.dot(hot, xbuf[...], preferred_element_type=F32).astype(BF)
 
     def zcopy(kind, step):
         peer = lax.rem(z + step, 4)
@@ -243,16 +271,21 @@
         remote(zsend.at[kind, peer], zrecv.at[kind, peer], z_send.at[kind, peer], z_recv.at[kind, peer], 2 * peer + y, m).wait_recv()
 
     for kind in range(3):
+        wlocal(kind).wait()
+        remote(weights[kind], wbuf.at[kind, other_y], w_send.at[kind], w_recv.at[kind], near, m).wait_recv()
+
         @pl.loop(0, 2)
         def _(tile):
             part = pl.ds(pl.multiple_of(tile * 256, 256), 256)
-            ysend[kind, part, :] = jnp.dot(
-                dense[other_y, part, :], weights[kind][...], preferred_element_type=F32).astype(BF)
-
-        ycopy(kind).start()
-
-    places = jnp.concatenate([
-        jnp.where(y == 0, auxbuf[b][1:2, 0:128], auxbuf[b][1:2, 128:256]) for b in range(8)], axis=1)
+            value = jnp.dot(
+                dense[part, :], wbuf[kind].reshape(1024, 512), preferred_element_type=F32).astype(BF)
+            for head in range(4):
+                zsend[kind, head, part, :] = value[:, head * 128:head * 128 + 128]
+
+        for step in range(1, 4):
+            zcopy(kind, step).start()
+
+    places = line_of(1)
     lanes = lax.broadcasted_iota(jnp.int32, (1, 128), 1) % 64
     freq = jnp.exp(-math.log(10000.0) * (2.0 * lanes.astype(F32) / 128))
     sign = jnp.where(lax.broadcasted_iota(jnp.int32, (1, 128), 1) < 64, -1.0, 1.0)
@@ -260,24 +293,10 @@
     @pl.loop(0, 4)
     def _(tile):
         part = pl.ds(pl.multiple_of(tile * 128, 128), 128)
-        where = jnp.sum(pick[y, part, :].astype(F32) * places, axis=1, keepdims=True)
+        where = jnp.sum(pick[part, :].astype(F32) * places, axis=1, keepdims=True)
         angle = where * freq
         cosine[part, :] = jnp.cos(angle)
         sine[part, :] = jnp.sin(angle) * sign
-
-    for kind in range(3):
-        ycopy(kind).wait_recv()
-
-        @pl.loop(0, 2)
-        def _(tile):
-            part = pl.ds(pl.multiple_of(tile * 256, 256), 256)
-            value = jnp.dot(dense[y, part, :], weights[kind][...], preferred_element_type=F32)
-            value = value + yrecv[kind, part, :].astype(F32)
-            for head in range(4):
-                zsend[kind, head, part, :] = value[:, head * 128:head * 128 + 128].astype(BF)
-
-        for step in range(1, 4):
-            zcopy(kind, step).start()
 
     def kvcopy(buf, kind):
         return remote(buf.at[y], buf.at[y], kv_send.at[kind], kv_recv.at[kind], near, m)
@@ -317,7 +336,7 @@
         att[part, :] = (summed / total).astype(BF)
 
     messages = lax.dot_general(
-        pick[y], att[...], (((0,), (0,)), ((), ())), preferred_element_type=F32)
+        pick[...], att[...], (((0,), (0,)), ((), ())), preferred_element_type=F32)
     msg[...] = messages.astype(BF).reshape(8, 128, 128)
     part = pl.ds(pl.multiple_of(y * 128, 128), 128)
     head = m * 4 + z
@@ -346,25 +365,27 @@
         other = lax.rem(m + step, 4)
         remote(stats.at[m], stats.at[m], st_send.at[step - 1], st_recv.at[m], s, other).wait_send()
     for half in range(2):
-        for across in range(2):
-            number = half * 2 + across
-            seq, mp = 2 * m + half, c + 2 * across
-
-            @pl.when(jnp.logical_not(jnp.logical_and(seq == s, mp == m)))
-            def _():
-                remote(nsend.at[half], xbuf.at[:, here, :], x_send.at[number], x_recv.at[s], seq, mp).wait_send()
-                remote(aux, auxbuf.at[s], a_send.at[number], a_recv.at[s], seq, mp).wait_send()
+        own, pair = xcopies(half)
+
+        @pl.when(jnp.logical_not(own))
+        def _():
+            for copy in pair:
+                copy.wait_send()
 
     @pl.when(direct)
     def _():
         @pl.loop(0, 8)
-        def _(block):
-            there = pl.ds(pl.multiple_of(block * 128, 128), 128)
-            remote(xbuf.at[:, there, :], xbuf.at[:, there, :], fx_send.at[block], x_recv.at[block], s, sibling).wait_send()
-            remote(auxbuf.at[block], auxbuf.at[block], fa_send.at[block], a_recv.at[block], s, sibling).wait_send()
+        def _(step):
+            for copy in forward(step, True)[1]:
+                copy.wait_send()
+
+            @pl.when(step < 4)
+            def _():
+                for copy in forward(step, False)[1]:
+                    copy.wait_send()
 
     for kind in range(3):
-        ycopy(kind).wait_send()
+        wcopy(kind).wait_send()
         for step in range(1, 4):
             zcopy(kind, step).wait_send()
     for kind, buf in enumerate((kbuf, vbuf)):
@@ -398,20 +419,22 @@
             jax.ShapeDtypeStruct((256, 128), F32),
             jax.ShapeDtypeStruct((256, 2048), BF),
         ),
-        in_specs=[pl.BlockSpec(memory_space=pltpu.VMEM)] * 7,
+        in_specs=[
+            pl.BlockSpec(memory_space=pltpu.VMEM), pl.BlockSpec(memory_space=pl.ANY),
+            pl.BlockSpec(memory_space=pltpu.VMEM), pl.BlockSpec(memory_space=pltpu.VMEM),
+        ] + [pl.BlockSpec(memory_space=pl.ANY)] * 3,
         out_specs=[pl.BlockSpec(memory_space=pltpu.VMEM)] * 3,
         scratch_shapes=[
+            pltpu.VMEM((1024, 1024), BF),
+            pltpu.VMEM((3, 2, 512, 512), BF),
             pltpu.VMEM((4, 8, 256), F32),
-            pltpu.VMEM((2, 2, 128, 512), BF),
+            pltpu.VMEM((256, 1024), BF),
             pltpu.VMEM((8, 256), F32),
-            pltpu.VMEM((2, 1024, 512), BF),
+            pltpu.VMEM((1024, 1024), BF),
             pltpu.VMEM((8, 8, 256), F32),
-            pltpu.VMEM((2, 512, 1024), BF),
-            pltpu.VMEM((2, 512, 512), BF),
-            pltpu.VMEM((3, 512, 512), BF),
-            pltpu.VMEM((3, 512, 512), BF),
+            pltpu.VMEM((512, 1024), BF),
+            pltpu.VMEM((512, 1024), BF),
             pltpu.VMEM((3, 4, 512, 128), BF),
-            pltpu.VMEM((8, 128), F32),
             pltpu.VMEM((3, 4, 512, 128), BF),
             pltpu.VMEM((512, 128), BF),
             pltpu.VMEM((2, 512, 128), BF),
@@ -421,8 +444,9 @@
             pltpu.VMEM((256, 2048), BF),
             pltpu.VMEM((512, 128), F32),
             pltpu.VMEM((512, 128), F32),
-            dma((3,)), dma((4,)), dma((4,)), dma((8,)), dma((4,)), dma((8,)), dma((8,)), dma((8,)),
-            dma((3,)), dma((3,)), dma((3, 4)), dma((3, 4)), dma((2,)), dma((2,)), dma((32,)), dma((32,)),
+            dma(()), dma((3,)), dma((3,)), dma((3,)),
+            dma((3,)), dma((4,)), dma((2,)), dma((8,)), dma((2,)), dma((8,)), dma((8,)), dma((8,)), dma((8,)), dma((8,)),
+            dma((3, 4)), dma((3, 4)), dma((2,)), dma((2,)), dma((32,)), dma((32,)),
         ],
         compiler_params=pltpu.CompilerParams(
             collective_id=0, has_side_effects=True, vmem_limit_bytes=48 * 2 ** 20),

time: 146 us -> 155 us (1.062)
  Pallas kernels: 139 us -> 148 us
    pallas_call x1, Pallas kernels: 133 us -> 142 us  [fused(): pl.pallas_call(mix_kernel, out_shape=(jax.ShapeDtypeStruct((256, 1024), B...]
where the time goes in v2:
time: 155 us
  Pallas kernels  148 us (95%)
  local copies, waits for them, and re-layouts  6.82 us (4%)
    pallas_call x1, Pallas kernels, fused(): pl.pallas_call(mix_kernel, out_shape=(jax.ShapeDtypeStruct((256, 1024), B...  142 us
    pallas_call x1, Pallas kernels, fused(): pl.pallas_call(finish_kernel, out_shape=jax.ShapeDtypeStruct((1024, 1024)...  5.74 us
    unnamed x10, local copies, waits for them, and re-layouts  5.4 us

profile of v2, /device:TPU:31, one launch (start us, length us, event | category | flops | bytes accessed | tf_op | source)
XLA Modules:
  0.0 154.9 jit_solution(15679520791901244114)
XLA Ops:
  0.0 0.7 reshape.10.gain_ref
  0.7 0.7 reshape.11.router_ref
  1.4 0.0 copy-start
  1.4 1.6 %copy-done = bf16[1024,1024]{1,0:T(8,128)(2,1)S(1)} copy-done((bf16[1024,1024]{1,0:T(8,128)(2,1)S(1)}, bf16[1024,1024]{1,0:T(8,128)(2,1)}, u32[]{:S(2)}) %copy-start) | copy-done | bytes 2097176
  3.0 0.0 copy-start.1
  3.0 1.0 copy-done.1
  4.1 0.0 copy-start.2
  4.1 1.0 copy-done.2
  5.1 0.0 copy-start.3
  5.1 1.0 copy-done.3
  6.1 0.0 copy-start.4
  6.1 0.7 copy-done.4
  6.8 142.3 %shard_map.82 = (bf16[256,1024]{1,0:T(8,128)(2,1)S(1)}, f32[256,128]{1,0:T(8,128)S(1)}, bf16[256,2048]{1,0:T(8,128)(2,1)S(1)}) custom-call(s32[1,1024]{1,0:T(1,128)S(1)} %bitcast.1, bf16[1024,1024]{1,0:T(8,128)(2,1)S(1)} %copy-done, f32[4,1024]{1,0:T(4,128)S(1)} %reshape.10.gain_ref, f32[4,1024]{1,0:T(4,128)S(1)} %reshape.11.router_ref, ...), custom_call_target="tpu_custom_call" | custom-call | tf_op jit(solution)/shard_map/pallas_call | solution.py:415
  149.2 5.7 %shard_map.83 = bf16[1024,1024]{1,0:T(8,128)(2,1)} custom-call(s32[1,1024]{1,0:T(1,128)S(1)} %bitcast.2, bf16[1024,1024]{1,0:T(8,128)(2,1)S(1)} %copy-done, bf16[256,1024]{1,0:T(8,128)(2,1)S(1)} %get-tuple-element.8.rows_ref, f32[256,128]{1,0:T(8,128)S(1)} %get-tuple-element.9.gate_ref, bf16[256,2048]{1,0:T(8,128)(2,1)S(1)} %get-tuple-element.10.att_ref, ...), custom_call_target="tpu_custom_call" | custom-call | tf_op jit(solution)/shard_map/pallas_call | solution.py:454
Async XLA Ops:
  1.4 1.6 %copy-start = (bf16[1024,1024]{1,0:T(8,128)(2,1)S(1)}, bf16[1024,1024]{1,0:T(8,128)(2,1)}, u32[]{:S(2)}) copy-start(bf16[1024,1024]{1,0:T(8,128)(2,1)} %hidden_ref.1) | copy-start | bytes 6291460
  3.0 1.0 copy-start.1
  4.1 1.0 copy-start.2
  5.1 1.0 copy-start.3
  6.1 0.7 copy-start.4

commit v3 on v2

--- a/solution.py
+++ b/solution.py
@@ -155,8 +155,7 @@
         return pltpu.make_async_copy(weights[kind], wbuf.at[kind, y], w_sem.at[kind])
 
     pl.semaphore_wait(barrier, 31)
-    for kind in range(3):
-        wcopy(kind).start()
+    wcopy(0).start()
     for kind in range(3):
         wlocal(kind).start()
     hidden_copy.wait()
@@ -248,6 +247,9 @@
         def _():
             for copy in pair:
                 copy.start()
+
+    for kind in (1, 2):
+        wcopy(kind).start()
 
     def line_of(which):
         return jnp.concatenate([jnp.where(

time: 155 us -> 122 us (0.79)
  Pallas kernels: 148 us -> 114 us
    pallas_call x1, Pallas kernels: 142 us -> 109 us  [fused(): pl.pallas_call(mix_kernel, out_shape=(jax.ShapeDtypeStruct((256, 1024), B...]
where the time goes in v3:
time: 122 us; the launch traced here: 121 us
  Pallas kernels  114 us (93%)
  local copies, waits for them, and re-layouts  6.82 us (6%)
    pallas_call x1, Pallas kernels, fused(): pl.pallas_call(mix_kernel, out_shape=(jax.ShapeDtypeStruct((256, 1024), B...  109 us
    pallas_call x1, Pallas kernels, fused(): pl.pallas_call(finish_kernel, out_shape=jax.ShapeDtypeStruct((1024, 1024)...  5.74 us
    unnamed x10, local copies, waits for them, and re-layouts  5.4 us

profile of v3, /device:TPU:31, one launch (start us, length us, event | category | flops | bytes accessed | tf_op | source)
XLA Modules:
  0.0 121.3 jit_solution(8192103076188758538)
XLA Ops:
  0.0 0.7 reshape.10.gain_ref
  0.7 0.7 reshape.11.router_ref
  1.4 0.0 copy-start
  1.4 1.6 %copy-done = bf16[1024,1024]{1,0:T(8,128)(2,1)S(1)} copy-done((bf16[1024,1024]{1,0:T(8,128)(2,1)S(1)}, bf16[1024,1024]{1,0:T(8,128)(2,1)}, u32[]{:S(2)}) %copy-start) | copy-done | bytes 2097176
  3.0 0.0 copy-start.1
  3.0 1.0 copy-done.1
  4.1 0.0 copy-start.2
  4.1 1.0 copy-done.2
  5.1 0.0 copy-start.3
  5.1 1.0 copy-done.3
  6.1 0.0 copy-start.4
  6.1 0.7 copy-done.4
  6.8 108.7 %shard_map.82 = (bf16[256,1024]{1,0:T(8,128)(2,1)S(1)}, f32[256,128]{1,0:T(8,128)S(1)}, bf16[256,2048]{1,0:T(8,128)(2,1)S(1)}) custom-call(s32[1,1024]{1,0:T(1,128)S(1)} %bitcast.1, bf16[1024,1024]{1,0:T(8,128)(2,1)S(1)} %copy-done, f32[4,1024]{1,0:T(4,128)S(1)} %reshape.10.gain_ref, f32[4,1024]{1,0:T(4,128)S(1)} %reshape.11.router_ref, ...), custom_call_target="tpu_custom_call" | custom-call | tf_op jit(solution)/shard_map/pallas_call | solution.py:417
  115.5 5.7 %shard_map.83 = bf16[1024,1024]{1,0:T(8,128)(2,1)} custom-call(s32[1,1024]{1,0:T(1,128)S(1)} %bitcast.2, bf16[1024,1024]{1,0:T(8,128)(2,1)S(1)} %copy-done, bf16[256,1024]{1,0:T(8,128)(2,1)S(1)} %get-tuple-element.8.rows_ref, f32[256,128]{1,0:T(8,128)S(1)} %get-tuple-element.9.gate_ref, bf16[256,2048]{1,0:T(8,128)(2,1)S(1)} %get-tuple-element.10.att_ref, ...), custom_call_target="tpu_custom_call" | custom-call | tf_op jit(solution)/shard_map/pallas_call | solution.py:456
Async XLA Ops:
  1.4 1.6 %copy-start = (bf16[1024,1024]{1,0:T(8,128)(2,1)S(1)}, bf16[1024,1024]{1,0:T(8,128)(2,1)}, u32[]{:S(2)}) copy-start(bf16[1024,1024]{1,0:T(8,128)(2,1)} %hidden_ref.1) | copy-start | bytes 6291460
  3.0 1.0 copy-start.1
  4.1 1.0 copy-start.2
  5.1 1.0 copy-start.3
  6.1 0.7 copy-start.4
